TPU v7x, 256 devices: a whole 4x4x8 slice. The times are simulated.
256 devices in a mesh: replica: 4 (over y), context: 32 (over x, z), tensor: 2 (over core).
Axes of the slice: x: 4, y: 4, z: 8, core: 2. Of those that a mesh axis runs over, the one named last changes fastest.
Arguments:
- query_nope: bfloat16 [4, 2, 4, 128, 128], P('replica', None, None, 'tensor'), may hold values from -9 to 9
- query_rope: bfloat16 [4, 2, 4, 128, 64], P('replica', None, None, 'tensor'), may hold values from -72 to 72
- key_map: bfloat16 [128, 512, 128], P('tensor', ('replica', 'context')), may hold values from -0.5 to 0.5
- value_map: bfloat16 [128, 512, 128], P('tensor', ('replica', 'context')), may hold values from -1.5 to 1.5
- out_map: bfloat16 [7168, 2, 64, 128], P(None, 'tensor', 'context'), may hold values from -0.09375 to 0.09375
- prompt_latent: bfloat16 [4, 131072, 512], P('replica', 'context'), may hold values from -6 to 6
- prompt_rope: bfloat16 [4, 64, 131072], P('replica', None, 'context'), may hold values from -6 to 6
- prompt_lengths: int32 [4], P('replica'), may hold values from 65536 to 131072, as said below
- suffix_latent: bfloat16 [4, 4, 128, 512], P('replica'), may hold values from -9 to 9
- suffix_rope: bfloat16 [4, 4, 64, 128], P('replica'), may hold values from -9 to 9
- suffix_lengths: int32 [4, 4], P('replica'), may hold values from 1 to 128, as said below
- new_latent: bfloat16 [4, 2, 4, 512], P('replica'), may hold values from -12 to 12
- new_rope: bfloat16 [4, 2, 4, 64], P('replica'), may hold values from -12 to 12
Outputs:
- mixed: bfloat16 [4, 7168, 2, 4], P('replica', ('context', 'tensor'))
Inputs may be any that keep to these rules, and one draw needn't show every extreme that they name: `prompt_lengths`: some prompt has all 131072 positions. `suffix_lengths`: some sample fills all 128 slots.
All inputs are finite; a program needn't handle non-finite values.
Results may differ from a plain program's by a relative error of at most 0.017.
Values may be sent and summed in bfloat16 or wider, within the bound.
A program may use at most 128 MiB of HBM per device.

v0:
```python
import jax
import jax.numpy as jnp
from jax import lax
from jax.sharding import PartitionSpec as P

masked_score = -1e30


def combined_all(x, axis, combine):
    everything = jax.tree.map(lambda part: lax.all_gather(part, axis), x)
    first = jax.tree.map(lambda part: part[0], everything)

    def lap(k, so_far):
        return combine(so_far, jax.tree.map(lambda part: part[k], everything))

    return lax.fori_loop(1, lax.axis_size(axis), lap, first)


def block_part(lat_rows, rope_rows, keys_here, rope_here, valid_keys, scaling):
    scores = lax.dot_general(
        lat_rows, keys_here, (((1,), (1,)), ((), ())), preferred_element_type=jnp.float32
    )
    scores = (scores + jnp.dot(rope_rows, rope_here, preferred_element_type=jnp.float32)) * scaling
    scores = jnp.where(valid_keys[None, :], scores, masked_score)
    row_max = jnp.max(scores, axis=1)
    exponent = jnp.where(valid_keys[None, :], jnp.exp(scores - row_max[:, None]), 0.0)
    row_sum = jnp.sum(exponent, axis=1)
    weighted = jnp.dot(exponent.astype(jnp.bfloat16), keys_here, preferred_element_type=jnp.float32)
    return (row_max, row_sum, weighted)


def join(former, latter):
    row_max = jnp.maximum(former[0], latter[0])
    former_scale = jnp.exp(former[0] - row_max)
    latter_scale = jnp.exp(latter[0] - row_max)
    return (
        row_max,
        former[1] * former_scale + latter[1] * latter_scale,
        former[2] * former_scale[..., None] + latter[2] * latter_scale[..., None],
    )


def recent_part(latent_q, rope_q, suffix_keys, suffix_rot, suffix_len, new_keys, new_rot, scaling):
    suffix_scores = jnp.einsum(
        "tshl,sil->tshi", latent_q, suffix_keys, preferred_element_type=jnp.float32
    )
    suffix_scores = (
        suffix_scores
        + jnp.einsum("tshr,sri->tshi", rope_q, suffix_rot, preferred_element_type=jnp.float32)
    ) * scaling
    new_scores = jnp.einsum(
        "tshl,usl->tshu", latent_q, new_keys, preferred_element_type=jnp.float32
    )
    new_scores = (
        new_scores
        + jnp.einsum("tshr,usr->tshu", rope_q, new_rot, preferred_element_type=jnp.float32)
    ) * scaling
    suffix_valid = (
        jnp.arange(suffix_keys.shape[1], dtype=jnp.int32)[None, :] < suffix_len[:, None]
    )[None, :, None, :]
    step_ids = jnp.arange(new_keys.shape[0], dtype=jnp.int32)
    new_valid = (step_ids[None, :] <= step_ids[:, None])[:, None, None, :]
    suffix_scores = jnp.where(suffix_valid, suffix_scores, masked_score)
    new_scores = jnp.where(new_valid, new_scores, masked_score)
    row_max = jnp.maximum(jnp.max(suffix_scores, axis=3), jnp.max(new_scores, axis=3))
    suffix_exp = jnp.where(suffix_valid, jnp.exp(suffix_scores - row_max[..., None]), 0.0)
    new_exp = jnp.where(new_valid, jnp.exp(new_scores - row_max[..., None]), 0.0)
    row_sum = jnp.sum(suffix_exp, axis=3) + jnp.sum(new_exp, axis=3)
    weighted = jnp.einsum(
        "tshi,sil->tshl",
        suffix_exp.astype(jnp.bfloat16),
        suffix_keys,
        preferred_element_type=jnp.float32,
    )
    weighted = weighted + jnp.einsum(
        "tshu,usl->tshl", new_exp.astype(jnp.bfloat16), new_keys, preferred_element_type=jnp.float32
    )
    return (row_max, row_sum, weighted)


def shards(
    query_nope,
    query_rope,
    key_map,
    value_map,
    out_map,
    prompt_latent,
    prompt_rope,
    prompt_lengths,
    suffix_latent,
    suffix_rope,
    suffix_lengths,
    new_latent,
    new_rope,
):
    step_count, sample_count, heads_here, nope_width = query_nope.shape[1:]
    rope_width = query_rope.shape[4]
    lat_width = prompt_latent.shape[2]
    prompt_here = prompt_latent.shape[1]
    scaling = (nope_width + rope_width) ** (-0.5)
    per_device = heads_here // lax.axis_size("context")
    first_head = lax.axis_index("context") * per_device
    nope_q = query_nope[0]
    rope_q = query_rope[0]
    own_rope = lax.dynamic_slice_in_dim(rope_q, first_head, per_device, 2)
    latent_q = jnp.einsum(
        "tshn,hln->tshl",
        nope_q,
        lax.all_gather(key_map, ("replica", "context"), axis=1, tiled=True),
        preferred_element_type=jnp.float32,
    ).astype(jnp.bfloat16)
    value_own = lax.all_to_all(value_map, "context", split_axis=0, concat_axis=1, tiled=True)
    value_full = lax.all_gather(value_own, "replica", axis=1, tiled=True)
    own_latent = lax.dynamic_slice_in_dim(latent_q, first_head, per_device, 2)
    positions = lax.axis_index("context") * prompt_here + jnp.arange(prompt_here, dtype=jnp.int32)
    valid_keys = positions < prompt_lengths[0]
    keys_here = prompt_latent[0]
    rope_here = prompt_rope[0]

    def step_part(step_pair):
        lat_rows = step_pair[0].reshape(-1, lat_width)
        rope_rows = step_pair[1].reshape(-1, rope_width)
        return block_part(lat_rows, rope_rows, keys_here, rope_here, valid_keys, scaling)

    row_max, row_sum, weighted = lax.map(step_part, (latent_q, rope_q))
    row_max = row_max.reshape(step_count, sample_count, heads_here)
    row_sum = row_sum.reshape(step_count, sample_count, heads_here)
    weighted = weighted.reshape(step_count, sample_count, heads_here, lat_width)
    merged = combined_all((row_max, row_sum, weighted), "context", join)
    prompt_part = tuple(
        (lax.dynamic_slice_in_dim(member, first_head, per_device, 2) for member in merged)
    )
    recent = recent_part(
        own_latent,
        own_rope,
        suffix_latent[0],
        suffix_rope[0],
        suffix_lengths[0],
        new_latent[0],
        new_rope[0],
        scaling,
    )
    row_max, row_sum, weighted = join(prompt_part, recent)
    latent_out = (weighted / row_sum[..., None]).astype(jnp.bfloat16)
    head_out = jnp.einsum(
        "tshl,hlv->tshv", latent_out, value_full, preferred_element_type=jnp.float32
    ).astype(jnp.bfloat16)
    flat_heads = head_out.reshape(step_count * sample_count, -1)
    out_rows = out_map.reshape(out_map.shape[0], -1)
    share_rows = out_rows.shape[0] // (lax.axis_size("context") * lax.axis_size("tensor"))
    mixed_out = lax.psum_scatter(
        lax.dot_general(
            out_rows, flat_heads, (((1,), (1,)), ((), ())), preferred_element_type=jnp.float32
        ),
        ("context", "tensor"),
        scatter_dimension=0,
        tiled=True,
    )
    return mixed_out.astype(jnp.bfloat16).reshape(1, share_rows, step_count, sample_count)


def solution(mesh):
    placed = (
        P("replica", None, None, "tensor", None),
        P("replica", None, None, "tensor", None),
        P("tensor", ("replica", "context"), None),
        P("tensor", ("replica", "context"), None),
        P(None, "tensor", "context", None),
        P("replica", "context", None),
        P("replica", None, "context"),
        P("replica"),
        P("replica", None, None, None),
        P("replica", None, None, None),
        P("replica", None),
        P("replica", None, None, None),
        P("replica", None, None, None),
    )
    return jax.shard_map(
        shards,
        mesh=mesh,
        in_specs=placed,
        out_specs=P("replica", ("context", "tensor"), None, None),
        check_vma=False,
    )
```

profile of v0, /device:TPU:1, one launch (start us, length us, event | category | flops | bytes accessed | tf_op | source)
XLA Modules:
  0.0 608.8 jit_solution(675710279868559705)
XLA Ops:
  6.5 1.5 copy.25
  8.2 127.8 %all-gather.3.cloned.1.call-done = bf16[64,512,128]{2,0,1:T(8,128)(2,1)} async-done(((bf16[64,4,128]{2,0,1:T(8,128)(2,1)}), bf16[64,512,128]{2,0,1:T(8,128)(2,1)}) %all-gather.3.cloned.1.call-update) | async-done | bytes 8388624 | tf_op jit(solution)/shard_map/all_gather | solution.py:109
  136.0 20.7 %fusion.25 = bf16[64,512,2,4]{1,3,2,0:T(4,128)(2,1)S(1)} fusion(bf16[64,512,128,1]{2,0,1,3:T(8,128)(2,1)} %bitcast.151, bf16[2,4,64,128]{3,2,1,0:T(8,128)(2,1)} %bitcast.152), kind=kOutput, calls=%fused_computation.30 | convolution fusion | flops 67371008 | bytes 9043968 | tf_op jit(solution)/shard_map/tshn,hln->tshl/dot_general | solution.py:106
  156.7 17.6 %while.35 = (s32[]{:T(128)}, f32[2,256]{1,0:T(2,128)S(1)}, f32[2,256]{1,0:T(2,128)S(1)}, f32[2,256,512]{2,1,0:T(8,128)S(1)}, bf16[2,4,64,512]{3,1,0,2:T(4,128)(2...) while((s32[]{:T(128)}, f32[2,256]{1,0:T(2,128)S(1)}, ...), condition=%wide.region_3.4_spmd.clone, body=%wide.region_0.3_spmd.clone.sunk | while | flops 2292194816 | bytes 48619692 | solution.py:125
  156.9 3.5 fusion.94
  165.7 3.5 fusion.94
  175.3 7.5 %all-to-all-start = ((bf16[64,4,128]{2,1,0:T(4,128)(2,1)}), bf16[64,4,128]{2,1,0:T(4,128)(2,1)S(1)}, u32[]{:S(2)}, u32[]{:S(2)}) async-start(bf16[64,4,128]{2,1,0:T(4,128)(2,1)} %param.20), calls=%async_computation | async-start | bytes 131072 | tf_op jit(solution)/shard_map/all_to_all | solution.py:112
  183.0 8.7 %all-to-all-done = bf16[64,4,128]{2,1,0:T(4,128)(2,1)S(1)} async-done(((bf16[64,4,128]{2,1,0:T(4,128)(2,1)}), bf16[64,4,128]{2,1,0:T(4,128)(2,1)S(1)}, u32[]{:S(2)}, u32[]{:S(2)}) %all-to-all-start) | async-done | bytes 65568 | tf_op jit(solution)/shard_map/all_to_all | solution.py:112
  191.8 10.6 %all_gather.19 = bf16[2,512,128]{2,1,0:T(8,128)(2,1)S(1)} all-gather(bf16[2,128,128]{2,1,0:T(8,128)(2,1)S(1)} %bitcast.146), channel_id=1, replica_groups=mesh['replica'=4,'context'=32,'tensor'=2] {'replica'}, dimensions={1}, use_global_device_ids=true | all-gather | bytes 327680 | tf_op jit(solution)/shard_map/all_gather | solution.py:113
  203.5 35.3 %all_gather.17 = f32[32,2,4,64]{3,2,1,0:T(4,128)S(1)} all-gather(f32[1,2,4,64]{3,2,1,0:T(4,128)S(1)} %all_gather_reshape.10), channel_id=1, replica_groups=mesh['replica'=4,'context'=32,'tensor'=2] {'context'}, dimensions={0}, use_global_device_ids=true | all-gather | bytes 67584 | tf_op jit(solution)/shard_map/all_gather | solution.py:10
  238.8 37.2 %all_gather.16 = f32[32,2,4,64]{3,2,1,0:T(4,128)S(1)} all-gather(f32[1,2,4,64]{3,2,1,0:T(4,128)S(1)} %all_gather_reshape.9), channel_id=1, replica_groups=mesh['replica'=4,'context'=32,'tensor'=2] {'context'}, dimensions={0}, use_global_device_ids=true | all-gather | bytes 67584 | tf_op jit(solution)/shard_map/all_gather | solution.py:10
  276.5 132.5 %all-gather.5.cloned.1.call-done = f32[32,2,4,64,512]{4,3,2,1,0:T(8,128)} async-done(((f32[1,2,4,64,512]{4,3,2,1,0:T(8,128)}), f32[32,2,4,64,512]{4,3,2,1,0:T(8,128)}) %all-gather.5.cloned.1.call-update) | async-done | bytes 33554448 | tf_op jit(solution)/shard_map/all_gather | solution.py:10
  410.3 49.0 %while.34 = (s32[]{:T(128)}, f32[2,4,64]{2,1,0:T(4,128)S(1)}, f32[2,4,64]{2,1,0:T(4,128)S(1)}, f32[2,4,64,512]{3,2,1,0:T(8,128)S(1)}, f32[32,2,4,64]{3,2,1,0:T(4...) while((s32[]{:T(128)}, f32[2,4,64]{2,1,0:T(4,128)S(1)}, ...), condition=%wide.region_5.6_spmd, body=%wide.region_4.5_spmd.sunk | while | flops 789509 | bytes 3166359 | solution.py:16
  410.3 1.5 fusion.87
  411.9 1.5 fusion.87
  413.5 1.5 fusion.87
  415.1 1.5 fusion.87
  416.6 1.5 fusion.87
  418.2 1.5 fusion.87
  419.8 1.5 fusion.87
  421.4 1.5 fusion.87
  423.0 1.5 fusion.87
  424.5 1.5 fusion.87
  426.1 1.5 fusion.87
  427.7 1.5 fusion.87
  429.3 1.5 fusion.87
  430.9 1.5 fusion.87
  432.4 1.5 fusion.87
  434.0 1.5 fusion.87
  435.6 1.5 fusion.87
  437.2 1.5 fusion.87
  438.8 1.5 fusion.87
  440.3 1.5 fusion.87
  441.9 1.5 fusion.87
  443.5 1.5 fusion.87
  445.1 1.5 fusion.87
  446.7 1.5 fusion.87
  448.2 1.5 fusion.87
  449.8 1.5 fusion.87
  451.4 1.5 fusion.87
  453.0 1.5 fusion.87
  454.6 1.5 fusion.87
  456.1 1.5 fusion.87
  457.7 1.5 fusion.87
  459.8 3.1 convolution_bitcast_fusion
  462.9 2.4 copy.56
  465.3 135.5 %reduce-scatter.4.cloned.1.call-done = f32[112,8]{1,0:T(8,128)} async-done(((f32[7168,8]{1,0:T(8,128)}), f32[112,8]{1,0:T(8,128)}) %reduce-scatter.4.cloned.1.call-update) | async-done | bytes 3600
  600.8 1.5 copy.57
  (104 shorter events, 16.0 us)
Async XLA Ops:
  6.5 196.5 %copy-start = (bf16[1,4,128,512]{3,2,1,0:T(8,128)(2,1)S(1)}, bf16[1,4,128,512]{3,2,1,0:T(8,128)(2,1)}, u32[]{:S(2)}) copy-start(bf16[1,4,128,512]{3,2,1,0:T(8,128)(2,1)} %param.25) | copy-start | bytes 1572868
  6.5 129.4 %all-gather.3.cloned.1.call-start = ((), (), s32[]{:S(2)}) async-start(), calls=%async_computation.2 | async-start | bytes 8454144 | tf_op jit(solution)/shard_map/all_gather | solution.py:109
  8.1 400.8 %all-gather.5.cloned.1.call-start = ((), (), s32[]{:S(2)}) async-start(), calls=%async_computation.3 | async-start | bytes 34603008 | tf_op jit(solution)/shard_map/all_gather | solution.py:10
  136.0 20.7 %copy-start.2 = (bf16[1,64,4096]{2,1,0:T(8,128)(2,1)S(1)}, bf16[1,64,4096]{2,1,0:T(8,128)(2,1)}, u32[]{:S(2)}) copy-start(bf16[1,64,4096]{2,1,0:T(8,128)(2,1)} %param.23) | copy-start | bytes 1572868
  136.0 20.7 %copy-start.4 = (bf16[1,2,4,64,64]{4,3,2,1,0:T(8,128)(2,1)S(1)}, bf16[1,2,4,64,64]{4,3,2,1,0:T(8,128)(2,1)}, u32[]{:S(2)}) copy-start(bf16[1,2,4,64,64]{4,3,2,1,0:T(8,128)(2,1)} %param.18) | copy-start | bytes 196612
  156.7 26.3 %copy-start.8 = (s32[1,4]{1,0:T(1,128)S(1)}, s32[1,4]{1,0:T(1,128)}, u32[]{:S(2)}) copy-start(s32[1,4]{1,0:T(1,128)} %param.27) | copy-start | bytes 52
  156.7 45.8 %copy-start.6 = (bf16[1,2,4,512]{3,2,1,0:T(4,128)(2,1)S(1)}, bf16[1,2,4,512]{3,2,1,0:T(4,128)(2,1)}, u32[]{:S(2)}) copy-start(bf16[1,2,4,512]{3,2,1,0:T(4,128)(2,1)} %param.28) | copy-start | bytes 24580
  156.7 46.1 %copy-start.7 = (bf16[1,2,4,64]{3,2,1,0:T(4,128)(2,1)S(1)}, bf16[1,2,4,64]{3,2,1,0:T(4,128)(2,1)}, u32[]{:S(2)}) copy-start(bf16[1,2,4,64]{3,2,1,0:T(4,128)(2,1)} %param.29) | copy-start | bytes 3076
  156.7 46.5 %copy-start.5 = (bf16[1,4,64,128]{3,2,1,0:T(8,128)(2,1)S(1)}, bf16[1,4,64,128]{3,2,1,0:T(8,128)(2,1)}, u32[]{:S(2)}) copy-start(bf16[1,4,64,128]{3,2,1,0:T(8,128)(2,1)} %param.26) | copy-start | bytes 196612
  161.1 2.2 copy-start.1
  169.9 2.2 copy-start.1
  174.3 1.0 copy-start.3
  175.3 16.4 %all-to-all-start = ((bf16[64,4,128]{2,1,0:T(4,128)(2,1)}), bf16[64,4,128]{2,1,0:T(4,128)(2,1)S(1)}, u32[]{:S(2)}, u32[]{:S(2)}) async-start(bf16[64,4,128]{2,1,0:T(4,128)(2,1)} %param.20), calls=%async_computation | async-start | bytes 131072 | tf_op jit(solution)/shard_map/all_to_all | solution.py:112
  182.9 417.9 %reduce-scatter.4.cloned.1.call-start = ((), (), s32[]{:S(2)}) async-start(), calls=%async_computation.4 | async-start | bytes 3727360
Sparse Core Ops, SparseCore 0:
  11.0 124.9 all-gather.2
  175.5 233.4 all-gather.4
  465.4 135.3 reduce-scatter.3
where the time goes:
time: 615 us; the launch traced here: 609 us
  waiting for transfers between devices  405 us (66%)
  blocking collectives  83.1 us (14%)
  other arithmetic  51.6 us (8%)
  matrix products  36.7 us (6%)
  between operations  13.3 us (2%)
  local copies, waits for them, and re-layouts  10.9 us (2%)
  starting transfers between devices  7.62 us (1%)
    unnamed x4, waiting for transfers between devices  136 us
    all_gather x1, waiting for transfers between devices, combined_all(): everything = jax.tree.map(lambda part: lax.all_gather(part, axis), x)  132 us
    all_gather x1, waiting for transfers between devices, shards(): lax.all_gather(key_map, ('replica', 'context'), axis=1, tiled=True)  128 us
    all_gather x2, blocking collectives, combined_all(): everything = jax.tree.map(lambda part: lax.all_gather(part, axis), x)  72.5 us
    add x31, other arithmetic, join(): former[2] * former_scale[..., None] + latter[2] * latter_scale[..., None]  47.3 us
    dot_general x1, matrix products, shards(): jnp.einsum('tshn,hln->tshl', nope_q, lax.all_gather(key_map, ('replica',...  20.7 us
  transfers between devices with their start and end apart: 4, of which 4 were waited for; matrix products, arithmetic and copies ran while one was open for 0% of the time, Pallas kernels for 0%

commit v1 on v0

v1 whole, which is shorter than its diff:
```python
import functools
import math

import jax
import jax.numpy as jnp
from jax import lax
from jax.experimental import pallas as pl
from jax.experimental.pallas import tpu as pltpu
from jax.sharding import PartitionSpec as P

MESH = pl.DeviceIdType.MESH
F32 = jnp.float32
BF16 = jnp.bfloat16
masked_score = -1e30

NY, NX, NZ = 4, 4, 8
LAT, NOPE, ROPE, VDIM = 512, 128, 64, 128
KEYS = 4096
ROWS = 512
GROUP = 128
WIDE = 640
FEATS = 112
SCALE2 = (NOPE + ROPE) ** -0.5 * math.log2(math.e)


def iota(shape, axis):
    return lax.broadcasted_iota(jnp.int32, shape, axis)


def dot(a, b, dims=((1,), (0,))):
    return lax.dot_general(a, b, (dims, ((), ())), preferred_element_type=F32)


def ones_where(mask):
    return jnp.where(mask, 1.0, 0.0).astype(BF16)


def split3(x):
    first = x.astype(BF16).astype(F32)
    second = (x - first).astype(BF16).astype(F32)
    return first, second, x - first - second


def pack_stats(top, total):
    lanes = iota((top.shape[0], 128), 1)
    packed = jnp.zeros((top.shape[0], 128), F32)
    for k, part in enumerate(split3(top) + split3(total)):
        packed = jnp.where(lanes == k, part, packed)
    return packed.astype(BF16)


def read_stats(packed):
    wide = packed.astype(F32)
    top = wide[:, 0:1] + wide[:, 1:2] + wide[:, 2:3]
    total = wide[:, 3:4] + wide[:, 4:5] + wide[:, 5:6]
    return top, total


def kernel(
    length_ref,
    suffix_length_ref,
    qn_hbm,
    qr_hbm,
    km_hbm,
    vm_hbm,
    om_hbm,
    keys_hbm,
    rope_hbm,
    sl_hbm,
    sr_hbm,
    nl_hbm,
    nr_hbm,
    out_ref,
    qn,
    qr,
    qnp,
    kmg,
    qslots,
    q,
    keys,
    kt,
    om,
    outs,
    v1,
    v3,
    vde,
    kr,
    sr,
    nl,
    nr,
    scores,
    fs,
    f1,
    f2s,
    f2,
    yb,
    yp,
    yx,
    yxs,
    yz,
    yzs,
    load_sem,
    b_send,
    b_recv,
    v_send,
    v_recv,
    dz_send,
    dz_recv,
    dx_send,
    dx_recv,
    f1_send,
    f1_recv,
    f2_send,
    f2_recv,
    h_send,
    h_recv,
):
    r = lax.axis_index("replica")
    c = lax.axis_index("context")
    t = lax.axis_index("tensor")
    x, z = c // NZ, c % NZ

    def at_y(o):
        return ((r + o) % NY, c, t)

    def at_x(o):
        return (r, ((x + o) % NX) * NZ + z, t)

    def at_z(o):
        return (r, x * NZ + (z + o) % NZ, t)

    other = (r, c, 1 - t)

    def remote(src, dst, send, recv, device):
        return pltpu.make_async_remote_copy(
            src_ref=src, dst_ref=dst, send_sem=send, recv_sem=recv, device_id=device, device_id_type=MESH
        )

    loads = [
        (qn_hbm, qn),
        (qr_hbm, qr),
        (km_hbm, kmg.at[r]),
        (vm_hbm.at[x], v1.at[x]),
        (keys_hbm, keys),
        (rope_hbm, kt.at[pl.ds(LAT, ROPE)]),
        (om_hbm, om),
        (sl_hbm, kr.at[pl.ds(0, 512)]),
        (sr_hbm, sr),
        (nl_hbm, nl),
        (nr_hbm, nr),
    ]
    copies = [pltpu.make_async_copy(a, b, load_sem.at[i]) for i, (a, b) in enumerate(loads)]
    for copy in copies:
        copy.start()

    barrier = pltpu.get_barrier_semaphore()
    peers = [at_y(o) for o in range(1, NY)] + [at_x(o) for o in range(1, NX)]
    peers += [at_z(o) for o in range(1, NZ)] + [other]
    for peer in peers:
        pl.semaphore_signal(barrier, inc=1, device_id=peer, device_id_type=MESH)
    pl.semaphore_wait(barrier, len(peers))

    sends = []

    def go(copy):
        copy.start()
        sends.append(copy)
        return copy

    b_copies = [go(remote(km_hbm, kmg.at[r], b_send.at[o], b_recv.at[o], at_y(o))) for o in range(1, NY)]
    va_copies = [
        go(remote(vm_hbm.at[(x + o) % NX], v1.at[x], v_send.at[o], v_recv.at[o], at_x(o))) for o in range(1, NX)
    ]

    copies[0].wait()
    copies[1].wait()
    order = ones_where(
        (iota((ROWS, ROWS), 0) // 8 == iota((ROWS, ROWS), 1) % 64)
        & (iota((ROWS, ROWS), 0) % 8 == iota((ROWS, ROWS), 1) // 64)
    )
    qnp[...] = dot(order, qn[...]).astype(BF16)
    widen = ones_where(iota((ROPE, 128), 0) == iota((ROPE, 128), 1))
    rope_rows = dot(order, dot(qr[...], widen).astype(BF16))
    q[:, LAT:WIDE] = jnp.where(iota((ROWS, 128), 1) == ROPE, 1.0, rope_rows).astype(BF16)

    position = c * KEYS + iota((64, KEYS), 1)
    beyond = (position >= length_ref[0]) & (iota((64, KEYS), 0) == 0)
    kt[LAT + ROPE : WIDE, :] = jnp.where(beyond, masked_score, 0.0).astype(BF16)
    copies[4].wait()

    @pl.loop(0, KEYS // 512)
    def _(i):
        rows = pl.ds(pl.multiple_of(i * 512, 512), 512)
        kt[0:LAT, rows] = keys[rows, :].T

    copies[5].wait()

    copies[2].wait()
    for copy in b_copies:
        copy.wait_recv()
    absorbed = dot(kmg[...].reshape(1024, NOPE), qnp[...], ((1,), (1,)))
    own_head = (iota((1024, ROWS), 0) // 4) % 64 == iota((1024, ROWS), 1) // 8
    absorbed = jnp.where(own_head, absorbed, 0.0).astype(BF16)
    pick = ones_where(
        (iota((16, 1024), 1) // 256 == iota((16, 1024), 0) // 4) & (iota((16, 1024), 1) % 4 == iota((16, 1024), 0) % 4)
    )
    qslots[c] = dot(pick, absorbed).astype(BF16)

    dz_copies = [
        go(remote(qslots.at[c], qslots.at[c], dz_send.at[o], dz_recv.at[o], at_z(o))) for o in range(1, NZ)
    ]
    dx_copies = []
    for i in range(NZ):
        if i:
            dz_copies[i - 1].wait_recv()
        slot = x * NZ + (z - i + NZ) % NZ
        for o in range(1, NX):
            k = i * 3 + o - 1
            dx_copies.append(go(remote(qslots.at[slot], qslots.at[slot], dx_send.at[k], dx_recv.at[k], at_x(o))))

    copies[3].wait()
    for copy in va_copies:
        copy.wait_recv()
    v3[r, :, z] = v1[:, z]
    vb_copies = [
        go(remote(v1.at[:, (z + o) % NZ], v3.at[r, :, z], v_send.at[3 + o], v_recv.at[3 + o], at_z(o)))
        for o in range(1, NZ)
    ]

    copies[6].wait()
    apart = ones_where(iota((256, 224), 1) == (iota((256, 224), 0) % 128) * 2 + iota((256, 224), 0) // 128)
    apart = jnp.where(iota((256, 224), 0) % 128 < FEATS, apart, jnp.zeros_like(apart))

    @pl.loop(0, 64)
    def _(d):
        both = dot(apart, om[d]).astype(BF16)
        outs[d, :, 0:128] = both[0:128]
        outs[d, :, 128:256] = both[128:256]

    for copy in vb_copies:
        copy.wait_recv()
    vc_copies = [
        go(remote(v3.at[r], v3.at[r], v_send.at[10 + o], v_recv.at[10 + o], at_y(o))) for o in range(1, NY)
    ]

    for copy in dx_copies:
        copy.wait_recv()
    row_of = iota((LAT, LAT), 0)
    line_up = ones_where(((row_of // 4) % 4) * 128 + (row_of // 16) * 4 + row_of % 4 == iota((LAT, LAT), 1))
    q[:, 0:LAT] = dot(qslots[...].reshape(LAT, ROWS), line_up, ((0,), (0,))).astype(BF16)

    f1_copies = []
    for i, o in enumerate((2, 1, 3, 0)):
        g = (x + o) % NX
        rows = pl.ds(pl.multiple_of(g * GROUP, GROUP), GROUP)
        q_rows = q[rows, :]
        top = None
        for k in range(KEYS // 512):
            cols = slice(k * 512, (k + 1) * 512)
            part = dot(q_rows, kt[:, cols])
            scores[:, cols] = part
            here = jnp.maximum(
                jnp.maximum(part[:, 0:128], part[:, 128:256]), jnp.maximum(part[:, 256:384], part[:, 384:512])
            )
            top = here if top is None else jnp.maximum(top, here)
        top = jnp.max(top, axis=1, keepdims=True)
        total = jnp.zeros((GROUP, 128), F32)
        weighted = jnp.zeros((GROUP, LAT), F32)
        for k in range(KEYS // 512):
            cols = slice(k * 512, (k + 1) * 512)
            e = jnp.exp2((scores[:, cols] - top) * SCALE2)
            total += e[:, 0:128] + e[:, 128:256] + e[:, 256:384] + e[:, 384:512]
            weighted += dot(e.astype(BF16), keys[cols, :])
        total = jnp.sum(total, axis=1, keepdims=True)
        if o:
            fs[i, :, 0:LAT] = weighted.astype(BF16)
            fs[i, :, LAT:WIDE] = pack_stats(top, total)
            f1_copies.append(go(remote(fs.at[i], f1.at[x], f1_send.at[i], f1_recv.at[i], at_x(o))))
        else:
            f1[x, :, 0:LAT] = weighted.astype(BF16)
            f1[x, :, LAT:WIDE] = pack_stats(top, total)

    for copy in f1_copies:
        copy.wait_recv()
    stats = [read_stats(f1[k, :, LAT:WIDE]) for k in range(NX)]
    top = functools.reduce(jnp.maximum, [s[0] for s in stats])
    factors = [jnp.exp2((s[0] - top) * SCALE2) for s in stats]
    total = sum(f * s[1] for f, s in zip(factors, stats))
    weighted = sum(f * f1[k, :, 0:LAT].astype(F32) for k, f in enumerate(factors))
    f2s[:, :, 0:LAT] = weighted.astype(BF16).reshape(NZ, 16, LAT)
    f2s[:, :, LAT:WIDE] = pack_stats(top, total).reshape(NZ, 16, 128)
    f2[z] = f2s[z]
    f2_copies = [
        go(remote(f2s.at[(z + o) % NZ], f2.at[z], f2_send.at[o], f2_recv.at[o], at_z(o))) for o in range(1, NZ)
    ]

    for i in (7, 8, 9, 10):
        copies[i].wait()
    place = ones_where(iota((128, 8), 0) == iota((128, 8), 1))
    kr[512:640, :] = dot(place, nl[...]).astype(BF16)
    new_rot = dot(place, nr[...]).astype(BF16)
    own = pl.ds(pl.multiple_of(c * 16, 16), 16)
    q_lat, q_rot = q[own, 0:LAT], q[own, LAT : LAT + ROPE]
    rot_scores = [dot(q_rot, sr[s]) for s in range(4)] + [dot(q_rot, new_rot, ((1,), (1,)))]
    recent = dot(q_lat, kr[...], ((1,), (1,))) + jnp.concatenate(rot_scores, axis=1)
    row, col = iota((16, WIDE), 0), iota((16, WIDE), 1)
    limit = jnp.zeros((16, WIDE), jnp.int32)
    for s in range(4):
        limit = jnp.where(col // 128 == s, suffix_length_ref[0, s], limit)
    suffix_valid = (col < 512) & (col // 128 == row % 4) & (col % 128 < limit)
    fresh = col - 512
    new_valid = (fresh >= 0) & (fresh < 8) & (fresh % 4 == row % 4) & (fresh // 4 <= (row // 4) % 2)
    valid = suffix_valid | new_valid
    recent = jnp.where(valid, recent, masked_score)
    recent_top = jnp.max(recent, axis=1, keepdims=True)
    e = jnp.where(valid, jnp.exp2((recent - recent_top) * SCALE2), 0.0)
    recent_total = jnp.sum(e, axis=1, keepdims=True)
    recent_sum = dot(e.astype(BF16), kr[...])

    for copy in vc_copies:
        copy.wait_recv()
    flat = v3[...].reshape(1024, VDIM)
    for k in range(2):
        latent = iota((LAT, 1024), 0)
        pick = ones_where(iota((LAT, 1024), 1) == (latent // 4) * 8 + k * 4 + latent % 4)
        vde[:, k * 128 : (k + 1) * 128] = dot(pick, flat).astype(BF16)

    for copy in f2_copies:
        copy.wait_recv()
    stats = [read_stats(f2[k, :, LAT:WIDE]) for k in range(NZ)]
    top = functools.reduce(jnp.maximum, [s[0] for s in stats] + [recent_top])
    factors = [jnp.exp2((s[0] - top) * SCALE2) for s in stats]
    recent_factor = jnp.exp2((recent_top - top) * SCALE2)
    total = sum(f * s[1] for f, s in zip(factors, stats)) + recent_factor * recent_total
    weighted = sum(f * f2[k, :, 0:LAT].astype(F32) for k, f in enumerate(factors)) + recent_factor * recent_sum
    latent_out = (weighted / total).astype(BF16)

    head_out = dot(latent_out, vde[...])
    head_out = jnp.concatenate([head_out[0:8, 0:128], head_out[8:16, 128:256]], axis=1).astype(BF16)
    for d in range(64):
        yb[d % 2, d // 2] = dot(head_out, outs[d], ((1,), (1,)))

    pair = go(remote(yb.at[1 - t], yp, h_send.at[0], h_recv.at[0], other))
    pair.wait_recv()
    yxs[...] = (yb[t] + yp[...]).reshape(NX, NZ, 8, 128)
    yx[x] = yxs[x]
    hx_copies = [
        go(remote(yxs.at[(x + o) % NX], yx.at[x], h_send.at[o], h_recv.at[o], at_x(o))) for o in range(1, NX)
    ]
    for copy in hx_copies:
        copy.wait_recv()
    yzs[...] = yx[0] + yx[1] + yx[2] + yx[3]
    yz[z] = yzs[z]
    hz_copies = [
        go(remote(yzs.at[(z + o) % NZ], yz.at[z], h_send.at[3 + o], h_recv.at[3 + o], at_z(o))) for o in range(1, NZ)
    ]
    for copy in hz_copies:
        copy.wait_recv()
    out_ref[...] = jnp.sum(yz[...], axis=0)

    for copy in sends:
        copy.wait_send()


def shards(
    query_nope,
    query_rope,
    key_map,
    value_map,
    out_map,
    prompt_latent,
    prompt_rope,
    prompt_lengths,
    suffix_latent,
    suffix_rope,
    suffix_lengths,
    new_latent,
    new_rope,
):
    any_spec = pl.BlockSpec(memory_space=pl.ANY)
    smem_spec = pl.BlockSpec(memory_space=pltpu.SMEM)
    dma = pltpu.SemaphoreType.DMA
    vmem = pltpu.VMEM
    summed = pl.pallas_call(
        kernel,
        out_shape=jax.ShapeDtypeStruct((8, 128), F32),
        in_specs=[smem_spec] * 2 + [any_spec] * 11,
        out_specs=pl.BlockSpec(memory_space=pltpu.VMEM),
        scratch_shapes=[
            vmem((ROWS, NOPE), BF16),
            vmem((ROWS, ROPE), BF16),
            vmem((ROWS, NOPE), BF16),
            vmem((NY, 256, NOPE), BF16),
            vmem((NX * NZ, 16, ROWS), BF16),
            vmem((ROWS, WIDE), BF16),
            vmem((KEYS, LAT), BF16),
            vmem((WIDE, KEYS), BF16),
            vmem((64, 224, VDIM), BF16),
            vmem((64, 128, 256), BF16),
            vmem((NX, NZ, 8, VDIM), BF16),
            vmem((NY, NX, NZ, 8, VDIM), BF16),
            vmem((LAT, 256), BF16),
            vmem((WIDE, LAT), BF16),
            vmem((4, ROPE, 128), BF16),
            vmem((8, LAT), BF16),
            vmem((8, ROPE), BF16),
            vmem((GROUP, KEYS), F32),
            vmem((3, GROUP, WIDE), BF16),
            vmem((NX, GROUP, WIDE), BF16),
            vmem((NZ, 16, WIDE), BF16),
            vmem((NZ, 16, WIDE), BF16),
            vmem((2, NX * NZ, 8, 128), F32),
            vmem((NX * NZ, 8, 128), F32),
            vmem((NX, NZ, 8, 128), F32),
            vmem((NX, NZ, 8, 128), F32),
            vmem((NZ, 8, 128), F32),
            vmem((NZ, 8, 128), F32),
            dma((11,)),
            dma((NY,)),
            dma((NY,)),
            dma((14,)),
            dma((14,)),
            dma((NZ,)),
            dma((NZ,)),
            dma((24,)),
            dma((24,)),
            dma((3,)),
            dma((3,)),
            dma((NZ,)),
            dma((NZ,)),
            dma((11,)),
            dma((11,)),
        ],
        compiler_params=pltpu.CompilerParams(
            collective_id=0, has_side_effects=True, vmem_limit_bytes=56 * 1024 * 1024
        ),
        name="latent_attention",
    )(
        prompt_lengths,
        suffix_lengths,
        query_nope.reshape(ROWS, NOPE),
        query_rope.reshape(ROWS, ROPE),
        key_map.reshape(256, NOPE),
        value_map.reshape(NX, NZ, 8, VDIM),
        out_map.reshape(64, 224, VDIM),
        prompt_latent[0],
        prompt_rope[0],
        suffix_latent.reshape(512, LAT),
        suffix_rope[0],
        new_latent.reshape(8, LAT),
        new_rope.reshape(8, ROPE),
    )
    return summed[:, :FEATS].T.astype(BF16).reshape(1, FEATS, 2, 4)


def solution(mesh):
    placed = (
        P("replica", None, None, "tensor", None),
        P("replica", None, None, "tensor", None),
        P("tensor", ("replica", "context"), None),
        P("tensor", ("replica", "context"), None),
        P(None, "tensor", "context", None),
        P("replica", "context", None),
        P("replica", None, "context"),
        P("replica"),
        P("replica", None, None, None),
        P("replica", None, None, None),
        P("replica", None),
        P("replica", None, None, None),
        P("replica", None, None, None),
    )
    return jax.shard_map(
        shards,
        mesh=mesh,
        in_specs=placed,
        out_specs=P("replica", ("context", "tensor"), None, None),
        check_vma=False,
    )
```

time: 615 us -> 66.9 us (0.11)
  waiting for transfers between devices: 405 us -> 0 us
  blocking collectives: 83.1 us -> 0 us
  Pallas kernels: 0 us -> 63.4 us
  other arithmetic: 51.6 us -> 1.25 us
  matrix products: 36.7 us -> 0 us
  between operations: 13.3 us -> 0.66 us
  local copies, waits for them, and re-layouts: 10.9 us -> 1.3 us
  starting transfers between devices: 7.62 us -> 0 us
    all_gather x2 -> x0, waiting for transfers between devices: 260 us -> none  [the longest x1 132 us: combined_all(): everything = jax.tree.map(lambda part: lax.all_gather(part, axis), x)]
    unnamed x4 -> x0, waiting for transfers between devices: 136 us -> none
    all_gather x3 -> x0, blocking collectives: 83.1 us -> none  [the longest x2 72.5 us: combined_all(): everything = jax.tree.map(lambda part: lax.all_gather(part, axis), x)]
    pallas_call x0 -> x1, Pallas kernels: none -> 63.4 us  [shards(): pl.pallas_call(kernel, out_shape=jax.ShapeDtypeStruct((8, 128), F32), in_...]
    add x63 -> x0, other arithmetic: 48.2 us -> none  [the longest x31 47.3 us: join(): former[2] * former_scale[..., None] + latter[2] * latter_scale[..., None]]
    dot_general x15 -> x0, matrix products: 36.7 us -> none  [the longest x1 20.7 us: shards(): jnp.einsum('tshn,hln->tshl', nope_q, lax.all_gather(key_map, ('replica',...]
    all_to_all x1 -> x0, waiting for transfers between devices: 8.7 us -> none  [shards(): lax.all_to_all(value_map, 'context', split_axis=0, concat_axis=1, tiled=T...]
    all_to_all x1 -> x0, starting transfers between devices: 7.53 us -> none  [shards(): lax.all_to_all(value_map, 'context', split_axis=0, concat_axis=1, tiled=T...]
  transfers between devices with their start and end apart: 4 -> 0, of which waited for: 4 -> 0; matrix products, arithmetic and copies ran while one was open for 0% -> 0% of each run, Pallas kernels for 0% -> 0%
where the time goes in v1:
time: 66.9 us; the launch traced here: 66.7 us
  Pallas kernels  63.4 us (95%)
  local copies, waits for them, and re-layouts  1.3 us (2%)
  other arithmetic  1.25 us (2%)
    pallas_call x1, Pallas kernels, shards(): pl.pallas_call(kernel, out_shape=jax.ShapeDtypeStruct((8, 128), F32), in_...  63.4 us

profile of v1, /device:TPU:1, one launch (start us, length us, event | category | flops | bytes accessed | tf_op | source)
XLA Modules:
  0.0 66.7 jit_solution(8133102075608585751)
XLA Ops:
  0.7 1.3 %reshape.33.nl_hbm = bf16[8,512]{1,0:T(8,128)(2,1)} reshape(bf16[1,2,4,512]{3,2,1,0:T(4,128)(2,1)} %param.24) | data formatting | bytes 16384 | tf_op jit(solution)/shard_map/reshape | solution.py:450
  2.0 63.4 %latent_attention.1 = f32[8,128]{1,0:T(8,128)} custom-call(s32[1]{0:T(128)S(6)} %copy.14.length_ref, s32[1,4]{1,0:T(1,128)} %suffix_length_ref.1, bf16[512,128]{1,0:T(8,128)(2,1)} %bitcast.18, bf16[512,64]{1,0:T(8,128)(2,1)} %bitcast.19, bf16[256,128]{1,0:T(8,128)(2,1)} %bitcast.20, bf16[4,8,8,128]{3,2,1,0:T(8,128)(2,1)} %bitcast.21, ...), custom_call_target="tpu_custom_call" | custom-call | tf_op jit(solution)/shard_map/latent_attention/pallas_call | solution.py:384
  65.4 1.3 %convert.3 = bf16[8,128]{1,0:T(8,128)(2,1)} convert(f32[8,128]{1,0:T(8,128)} %latent_attention.1) | non-fusion elementwise | flops 1024 | bytes 6144 | tf_op jit(solution)/shard_map/convert

commit v2 on v1

--- a/solution.py
+++ b/solution.py
@@ -94,9 +94,7 @@
     f2s,
     f2,
     yb,
-    yp,
     yx,
-    yxs,
     yz,
     yzs,
     load_sem,
@@ -123,13 +121,11 @@
     def at_y(o):
         return ((r + o) % NY, c, t)
 
-    def at_x(o):
-        return (r, ((x + o) % NX) * NZ + z, t)
+    def at_x(o, core=t):
+        return (r, ((x + o) % NX) * NZ + z, core)
 
     def at_z(o):
         return (r, x * NZ + (z + o) % NZ, t)
-
-    other = (r, c, 1 - t)
 
     def remote(src, dst, send, recv, device):
         return pltpu.make_async_remote_copy(
@@ -139,11 +135,11 @@
     loads = [
         (qn_hbm, qn),
         (qr_hbm, qr),
+        (keys_hbm, keys),
+        (om_hbm, om),
         (km_hbm, kmg.at[r]),
+        (rope_hbm, kt.at[pl.ds(LAT, ROPE)]),
         (vm_hbm.at[x], v1.at[x]),
-        (keys_hbm, keys),
-        (rope_hbm, kt.at[pl.ds(LAT, ROPE)]),
-        (om_hbm, om),
         (sl_hbm, kr.at[pl.ds(0, 512)]),
         (sr_hbm, sr),
         (nl_hbm, nl),
@@ -155,22 +151,9 @@
 
     barrier = pltpu.get_barrier_semaphore()
     peers = [at_y(o) for o in range(1, NY)] + [at_x(o) for o in range(1, NX)]
-    peers += [at_z(o) for o in range(1, NZ)] + [other]
+    peers += [at_x(o, 1 - t) for o in range(NX)] + [at_z(o) for o in range(1, NZ)]
     for peer in peers:
         pl.semaphore_signal(barrier, inc=1, device_id=peer, device_id_type=MESH)
-    pl.semaphore_wait(barrier, len(peers))
-
-    sends = []
-
-    def go(copy):
-        copy.start()
-        sends.append(copy)
-        return copy
-
-    b_copies = [go(remote(km_hbm, kmg.at[r], b_send.at[o], b_recv.at[o], at_y(o))) for o in range(1, NY)]
-    va_copies = [
-        go(remote(vm_hbm.at[(x + o) % NX], v1.at[x], v_send.at[o], v_recv.at[o], at_x(o))) for o in range(1, NX)
-    ]
 
     copies[0].wait()
     copies[1].wait()
@@ -186,16 +169,39 @@
     position = c * KEYS + iota((64, KEYS), 1)
     beyond = (position >= length_ref[0]) & (iota((64, KEYS), 0) == 0)
     kt[LAT + ROPE : WIDE, :] = jnp.where(beyond, masked_score, 0.0).astype(BF16)
-    copies[4].wait()
+    copies[2].wait()
 
     @pl.loop(0, KEYS // 512)
     def _(i):
         rows = pl.ds(pl.multiple_of(i * 512, 512), 512)
         kt[0:LAT, rows] = keys[rows, :].T
 
-    copies[5].wait()
-
-    copies[2].wait()
+    copies[3].wait()
+    apart = ones_where(iota((256, 224), 1) == (iota((256, 224), 0) % 128) * 2 + iota((256, 224), 0) // 128)
+    apart = jnp.where(iota((256, 224), 0) % 128 < FEATS, apart, jnp.zeros_like(apart))
+
+    @pl.loop(0, 64, step=8)
+    def _(first):
+        for d in range(8):
+            both = dot(apart, om[first + d]).astype(BF16)
+            outs[first + d, :, 0:128] = both[0:128]
+            outs[first + d, :, 128:256] = both[128:256]
+
+    pl.semaphore_wait(barrier, len(peers))
+
+    sends = []
+
+    def go(copy):
+        copy.start()
+        sends.append(copy)
+        return copy
+
+    b_copies = [go(remote(km_hbm, kmg.at[r], b_send.at[o], b_recv.at[o], at_y(o))) for o in range(1, NY)]
+    va_copies = [
+        go(remote(vm_hbm.at[(x + o) % NX], v1.at[x], v_send.at[o], v_recv.at[o], at_x(o))) for o in range(1, NX)
+    ]
+
+    copies[4].wait()
     for copy in b_copies:
         copy.wait_recv()
     absorbed = dot(kmg[...].reshape(1024, NOPE), qnp[...], ((1,), (1,)))
@@ -204,21 +210,42 @@
     pick = ones_where(
         (iota((16, 1024), 1) // 256 == iota((16, 1024), 0) // 4) & (iota((16, 1024), 1) % 4 == iota((16, 1024), 0) % 4)
     )
-    qslots[c] = dot(pick, absorbed).astype(BF16)
-
-    dz_copies = [
-        go(remote(qslots.at[c], qslots.at[c], dz_send.at[o], dz_recv.at[o], at_z(o))) for o in range(1, NZ)
-    ]
-    dx_copies = []
-    for i in range(NZ):
+    piece = dot(pick, absorbed).astype(BF16)
+    qslots[0, c] = piece[:, 0:256]
+    qslots[1, c] = piece[:, 256:512]
+
+    def slots(half, first, count=1):
+        return qslots.at[half, pl.ds(first, count)]
+
+    dz_copies = {
+        o: go(
+            remote(qslots.at[:, c], qslots.at[:, c], dz_send.at[o], dz_recv.at[o], at_z(o))
+        )
+        for o in (4, 3, 5, 2, 6, 1, 7)
+    }
+    early_copies, late_copies = [], []
+    for k, i in enumerate((0, 1, 7, 2, 6, 3, 5, 4)):
         if i:
-            dz_copies[i - 1].wait_recv()
+            dz_copies[i].wait_recv()
         slot = x * NZ + (z - i + NZ) % NZ
-        for o in range(1, NX):
-            k = i * 3 + o - 1
-            dx_copies.append(go(remote(qslots.at[slot], qslots.at[slot], dx_send.at[k], dx_recv.at[k], at_x(o))))
-
-    copies[3].wait()
+        for o in (2, 1, 3):
+            half = 1 - ((x + o) % NX) // 2
+            n = k * 3 + o - 1
+            early_copies.append(
+                go(remote(slots(half, slot), slots(half, slot), dx_send.at[n], dx_recv.at[n], at_x(o)))
+            )
+    for o in (2, 1, 3):
+        half = ((x + o) % NX) // 2
+        n = 23 + o
+        late_copies.append(
+            go(
+                remote(
+                    slots(half, x * NZ, NZ), slots(half, x * NZ, NZ), dx_send.at[n], dx_recv.at[n], at_x(o)
+                )
+            )
+        )
+
+    copies[6].wait()
     for copy in va_copies:
         copy.wait_recv()
     v3[r, :, z] = v1[:, z]
@@ -227,30 +254,18 @@
         for o in range(1, NZ)
     ]
 
-    copies[6].wait()
-    apart = ones_where(iota((256, 224), 1) == (iota((256, 224), 0) % 128) * 2 + iota((256, 224), 0) // 128)
-    apart = jnp.where(iota((256, 224), 0) % 128 < FEATS, apart, jnp.zeros_like(apart))
-
-    @pl.loop(0, 64)
-    def _(d):
-        both = dot(apart, om[d]).astype(BF16)
-        outs[d, :, 0:128] = both[0:128]
-        outs[d, :, 128:256] = both[128:256]
-
-    for copy in vb_copies:
-        copy.wait_recv()
-    vc_copies = [
-        go(remote(v3.at[r], v3.at[r], v_send.at[10 + o], v_recv.at[10 + o], at_y(o))) for o in range(1, NY)
-    ]
-
-    for copy in dx_copies:
-        copy.wait_recv()
+    copies[5].wait()
     row_of = iota((LAT, LAT), 0)
     line_up = ones_where(((row_of // 4) % 4) * 128 + (row_of // 16) * 4 + row_of % 4 == iota((LAT, LAT), 1))
-    q[:, 0:LAT] = dot(qslots[...].reshape(LAT, ROWS), line_up, ((0,), (0,))).astype(BF16)
-
     f1_copies = []
-    for i, o in enumerate((2, 1, 3, 0)):
+    for i in range(NX):
+        o = (2, 3 - 2 * (x % 2), 1 + 2 * (x % 2), 0)[i]
+        if i % 2 == 0:
+            for copy in (late_copies if i else early_copies):
+                copy.wait_recv()
+            half = x // 2 if i else 1 - x // 2
+            gathered = dot(qslots[half].reshape(LAT, 256), line_up, ((0,), (0,)))
+            q[pl.ds(pl.multiple_of(half * 256, 256), 256), 0:LAT] = gathered.astype(BF16)
         g = (x + o) % NX
         rows = pl.ds(pl.multiple_of(g * GROUP, GROUP), GROUP)
         q_rows = q[rows, :]
@@ -272,32 +287,42 @@
             total += e[:, 0:128] + e[:, 128:256] + e[:, 256:384] + e[:, 384:512]
             weighted += dot(e.astype(BF16), keys[cols, :])
         total = jnp.sum(total, axis=1, keepdims=True)
-        if o:
+        if i < NX - 1:
             fs[i, :, 0:LAT] = weighted.astype(BF16)
             fs[i, :, LAT:WIDE] = pack_stats(top, total)
-            f1_copies.append(go(remote(fs.at[i], f1.at[x], f1_send.at[i], f1_recv.at[i], at_x(o))))
+            f1_copies.append(go(remote(fs.at[i], f1.at[x], f1_send.at[o], f1_recv.at[o], at_x(o))))
         else:
             f1[x, :, 0:LAT] = weighted.astype(BF16)
             f1[x, :, LAT:WIDE] = pack_stats(top, total)
+        if i == 1:
+            for copy in vb_copies:
+                copy.wait_recv()
+            vc_copies = [
+                go(remote(v3.at[r], v3.at[r], v_send.at[10 + o], v_recv.at[10 + o], at_y(o)))
+                for o in range(1, NY)
+            ]
 
     for copy in f1_copies:
         copy.wait_recv()
-    stats = [read_stats(f1[k, :, LAT:WIDE]) for k in range(NX)]
-    top = functools.reduce(jnp.maximum, [s[0] for s in stats])
-    factors = [jnp.exp2((s[0] - top) * SCALE2) for s in stats]
-    total = sum(f * s[1] for f, s in zip(factors, stats))
-    weighted = sum(f * f1[k, :, 0:LAT].astype(F32) for k, f in enumerate(factors))
-    f2s[:, :, 0:LAT] = weighted.astype(BF16).reshape(NZ, 16, LAT)
-    f2s[:, :, LAT:WIDE] = pack_stats(top, total).reshape(NZ, 16, 128)
-    f2[z] = f2s[z]
-    f2_copies = [
-        go(remote(f2s.at[(z + o) % NZ], f2.at[z], f2_send.at[o], f2_recv.at[o], at_z(o))) for o in range(1, NZ)
-    ]
+    f2_copies = []
+    for o in (4, 3, 5, 2, 6, 1, 7, 0):
+        there = (z + o) % NZ
+        rows = pl.ds(pl.multiple_of(there * 16, 16), 16)
+        stats = [read_stats(f1[k, rows, LAT:WIDE]) for k in range(NX)]
+        top = functools.reduce(jnp.maximum, [s[0] for s in stats])
+        factors = [jnp.exp2((s[0] - top) * SCALE2) for s in stats]
+        total = sum(f * s[1] for f, s in zip(factors, stats))
+        weighted = sum(f * f1[k, rows, 0:LAT].astype(F32) for k, f in enumerate(factors))
+        place = f2s if o else f2
+        place[there, :, 0:LAT] = weighted.astype(BF16)
+        place[there, :, LAT:WIDE] = pack_stats(top, total)
+        if o:
+            f2_copies.append(go(remote(f2s.at[there], f2.at[z], f2_send.at[o], f2_recv.at[o], at_z(o))))
 
     for i in (7, 8, 9, 10):
         copies[i].wait()
     place = ones_where(iota((128, 8), 0) == iota((128, 8), 1))
-    kr[512:640, :] = dot(place, nl[...]).astype(BF16)
+    kr[512:640, :] = (dot(place[:, 0:4], nl[0]) + dot(place[:, 4:8], nl[1])).astype(BF16)
     new_rot = dot(place, nr[...]).astype(BF16)
     own = pl.ds(pl.multiple_of(c * 16, 16), 16)
     q_lat, q_rot = q[own, 0:LAT], q[own, LAT : LAT + ROPE]
@@ -337,22 +362,25 @@
 
     head_out = dot(latent_out, vde[...])
     head_out = jnp.concatenate([head_out[0:8, 0:128], head_out[8:16, 128:256]], axis=1).astype(BF16)
-    for d in range(64):
-        yb[d % 2, d // 2] = dot(head_out, outs[d], ((1,), (1,)))
-
-    pair = go(remote(yb.at[1 - t], yp, h_send.at[0], h_recv.at[0], other))
-    pair.wait_recv()
-    yxs[...] = (yb[t] + yp[...]).reshape(NX, NZ, 8, 128)
-    yx[x] = yxs[x]
-    hx_copies = [
-        go(remote(yxs.at[(x + o) % NX], yx.at[x], h_send.at[o], h_recv.at[o], at_x(o))) for o in range(1, NX)
-    ]
+    hx_copies = []
+    for o, away in ((2, 1), (2, 0), (1, 1), (1, 0), (3, 1), (3, 0), (0, 1), (0, 0)):
+        there, core = (x + o) % NX, (t + away) % 2
+        for k in range(0, NZ, 2):
+            first = (there * NZ + k) * 2 + core
+            part = [dot(head_out, outs[first + 2 * m], ((1,), (1,))) for m in range(2)]
+            place = yb if o or away else yx
+            place[there, core, k * 8 : k * 8 + 16] = jnp.concatenate(part, axis=0).astype(BF16)
+        if o or away:
+            n = o * 2 + away
+            hx_copies.append(go(remote(yb.at[there, core], yx.at[x, t], h_send.at[n], h_recv.at[n], at_x(o, core))))
     for copy in hx_copies:
         copy.wait_recv()
-    yzs[...] = yx[0] + yx[1] + yx[2] + yx[3]
+    own_sum = sum(yx[k, core].astype(F32) for k in range(NX) for core in range(2))
+    yzs[...] = own_sum.reshape(NZ, 8, 128)
     yz[z] = yzs[z]
     hz_copies = [
-        go(remote(yzs.at[(z + o) % NZ], yz.at[z], h_send.at[3 + o], h_recv.at[3 + o], at_z(o))) for o in range(1, NZ)
+        go(remote(yzs.at[(z + o) % NZ], yz.at[z], h_send.at[7 + o], h_recv.at[7 + o], at_z(o)))
+        for o in (4, 3, 5, 2, 6, 1, 7)
     ]
     for copy in hz_copies:
         copy.wait_recv()
@@ -391,7 +419,7 @@
             vmem((ROWS, ROPE), BF16),
             vmem((ROWS, NOPE), BF16),
             vmem((NY, 256, NOPE), BF16),
-            vmem((NX * NZ, 16, ROWS), BF16),
+            vmem((2, NX * NZ, 16, 256), BF16),
             vmem((ROWS, WIDE), BF16),
             vmem((KEYS, LAT), BF16),
             vmem((WIDE, KEYS), BF16),
@@ -402,17 +430,15 @@
             vmem((LAT, 256), BF16),
             vmem((WIDE, LAT), BF16),
             vmem((4, ROPE, 128), BF16),
-            vmem((8, LAT), BF16),
+            vmem((2, 4, LAT), BF16),
             vmem((8, ROPE), BF16),
             vmem((GROUP, KEYS), F32),
             vmem((3, GROUP, WIDE), BF16),
             vmem((NX, GROUP, WIDE), BF16),
             vmem((NZ, 16, WIDE), BF16),
             vmem((NZ, 16, WIDE), BF16),
-            vmem((2, NX * NZ, 8, 128), F32),
-            vmem((NX * NZ, 8, 128), F32),
-            vmem((NX, NZ, 8, 128), F32),
-            vmem((NX, NZ, 8, 128), F32),
+            vmem((NX, 2, NZ * 8, 128), BF16),
+            vmem((NX, 2, NZ * 8, 128), BF16),
             vmem((NZ, 8, 128), F32),
             vmem((NZ, 8, 128), F32),
             dma((11,)),
@@ -422,14 +448,14 @@
             dma((14,)),
             dma((NZ,)),
             dma((NZ,)),
-            dma((24,)),
-            dma((24,)),
-            dma((3,)),
-            dma((3,)),
+            dma((27,)),
+            dma((27,)),
+            dma((NX,)),
+            dma((NX,)),
             dma((NZ,)),
             dma((NZ,)),
-            dma((11,)),
-            dma((11,)),
+            dma((15,)),
+            dma((15,)),
         ],
         compiler_params=pltpu.CompilerParams(
             collective_id=0, has_side_effects=True, vmem_limit_bytes=56 * 1024 * 1024
@@ -447,7 +473,7 @@
         prompt_rope[0],
         suffix_latent.reshape(512, LAT),
         suffix_rope[0],
-        new_latent.reshape(8, LAT),
+        new_latent[0],
         new_rope.reshape(8, ROPE),
     )
     return summed[:, :FEATS].T.astype(BF16).reshape(1, FEATS, 2, 4)

time: 66.9 us -> 59.3 us (0.89)
  Pallas kernels: 63.4 us -> 57.2 us
  local copies, waits for them, and re-layouts: 1.3 us -> 0 us
    pallas_call x1, Pallas kernels: 63.4 us -> 57.2 us  [shards(): pl.pallas_call(kernel, out_shape=jax.ShapeDtypeStruct((8, 128), F32), in_...]
    reshape x1 -> x0, local copies, waits for them, and re-layouts: 1.3 us -> none  [shards(): new_latent.reshape(8, LAT)]
where the time goes in v2:
time: 59.3 us; the launch traced here: 59.1 us
  Pallas kernels  57.2 us (96%)
  other arithmetic  1.26 us (2%)
  between operations  0.66 us (1%)
    pallas_call x1, Pallas kernels, shards(): pl.pallas_call(kernel, out_shape=jax.ShapeDtypeStruct((8, 128), F32), in_...  57.2 us
    another operation x1, other arithmetic  1.26 us

profile of v2, /device:TPU:1, one launch (start us, length us, event | category | flops | bytes accessed | tf_op | source)
XLA Modules:
  0.0 59.1 jit_solution(3854712967158808716)
XLA Ops:
  0.7 57.2 %latent_attention.1 = f32[8,128]{1,0:T(8,128)} custom-call(s32[1]{0:T(128)S(6)} %copy.14.length_ref, s32[1,4]{1,0:T(1,128)} %suffix_length_ref.1, bf16[512,128]{1,0:T(8,128)(2,1)} %bitcast.19, bf16[512,64]{1,0:T(8,128)(2,1)} %bitcast.20, bf16[256,128]{1,0:T(8,128)(2,1)} %bitcast.21, bf16[4,8,8,128]{3,2,1,0:T(8,128)(2,1)} %bitcast.22, ...), custom_call_target="tpu_custom_call" | custom-call | tf_op jit(solution)/shard_map/latent_attention/pallas_call | solution.py:412
  57.9 1.3 %convert.3 = bf16[8,128]{1,0:T(8,128)(2,1)} convert(f32[8,128]{1,0:T(8,128)} %latent_attention.1) | non-fusion elementwise | flops 1024 | bytes 6144 | tf_op jit(solution)/shard_map/convert

commit v3 on v2

--- a/solution.py
+++ b/solution.py
@@ -57,8 +57,8 @@
 
 
 def kernel(
-    length_ref,
-    suffix_length_ref,
+    length_hbm,
+    suffix_length_hbm,
     qn_hbm,
     qr_hbm,
     km_hbm,
@@ -97,6 +97,8 @@
     yx,
     yz,
     yzs,
+    length_ref,
+    suffix_length_ref,
     load_sem,
     b_send,
     b_recv,
@@ -144,6 +146,8 @@
         (sr_hbm, sr),
         (nl_hbm, nl),
         (nr_hbm, nr),
+        (length_hbm, length_ref),
+        (suffix_length_hbm, suffix_length_ref),
     ]
     copies = [pltpu.make_async_copy(a, b, load_sem.at[i]) for i, (a, b) in enumerate(loads)]
     for copy in copies:
@@ -154,6 +158,21 @@
     peers += [at_x(o, 1 - t) for o in range(NX)] + [at_z(o) for o in range(1, NZ)]
     for peer in peers:
         pl.semaphore_signal(barrier, inc=1, device_id=peer, device_id_type=MESH)
+
+    pl.semaphore_wait(barrier, len(peers))
+
+    sends = []
+
+    def go(copy):
+        copy.start()
+        sends.append(copy)
+        return copy
+
+    copies[4].wait()
+    b_copies = [go(remote(kmg.at[r], kmg.at[r], b_send.at[o], b_recv.at[o], at_y(o))) for o in range(1, NY)]
+    va_copies = [
+        go(remote(vm_hbm.at[(x + o) % NX], v1.at[x], v_send.at[o], v_recv.at[o], at_x(o))) for o in range(1, NX)
+    ]
 
     copies[0].wait()
     copies[1].wait()
@@ -166,6 +185,7 @@
     rope_rows = dot(order, dot(qr[...], widen).astype(BF16))
     q[:, LAT:WIDE] = jnp.where(iota((ROWS, 128), 1) == ROPE, 1.0, rope_rows).astype(BF16)
 
+    copies[11].wait()
     position = c * KEYS + iota((64, KEYS), 1)
     beyond = (position >= length_ref[0]) & (iota((64, KEYS), 0) == 0)
     kt[LAT + ROPE : WIDE, :] = jnp.where(beyond, masked_score, 0.0).astype(BF16)
@@ -176,32 +196,29 @@
         rows = pl.ds(pl.multiple_of(i * 512, 512), 512)
         kt[0:LAT, rows] = keys[rows, :].T
 
+    copies[6].wait()
+    for copy in va_copies:
+        copy.wait_recv()
+    v3[r, :, z] = v1[:, z]
+    vb_copies = [
+        go(remote(v1.at[:, (z + o) % NZ], v3.at[r, :, z], v_send.at[3 + o], v_recv.at[3 + o], at_z(o)))
+        for o in range(1, NZ)
+    ]
+
     copies[3].wait()
     apart = ones_where(iota((256, 224), 1) == (iota((256, 224), 0) % 128) * 2 + iota((256, 224), 0) // 128)
     apart = jnp.where(iota((256, 224), 0) % 128 < FEATS, apart, jnp.zeros_like(apart))
 
-    @pl.loop(0, 64, step=8)
-    def _(first):
-        for d in range(8):
-            both = dot(apart, om[first + d]).astype(BF16)
-            outs[first + d, :, 0:128] = both[0:128]
-            outs[first + d, :, 128:256] = both[128:256]
-
-    pl.semaphore_wait(barrier, len(peers))
-
-    sends = []
-
-    def go(copy):
-        copy.start()
-        sends.append(copy)
-        return copy
-
-    b_copies = [go(remote(km_hbm, kmg.at[r], b_send.at[o], b_recv.at[o], at_y(o))) for o in range(1, NY)]
-    va_copies = [
-        go(remote(vm_hbm.at[(x + o) % NX], v1.at[x], v_send.at[o], v_recv.at[o], at_x(o))) for o in range(1, NX)
-    ]
-
-    copies[4].wait()
+    def take_apart(begin, end):
+        @pl.loop(begin, end, step=8)
+        def _(first):
+            for d in range(8):
+                both = dot(apart, om[first + d]).astype(BF16)
+                outs[first + d, :, 0:128] = both[0:128]
+                outs[first + d, :, 128:256] = both[128:256]
+
+    take_apart(0, 24)
+
     for copy in b_copies:
         copy.wait_recv()
     absorbed = dot(kmg[...].reshape(1024, NOPE), qnp[...], ((1,), (1,)))
@@ -211,61 +228,36 @@
         (iota((16, 1024), 1) // 256 == iota((16, 1024), 0) // 4) & (iota((16, 1024), 1) % 4 == iota((16, 1024), 0) % 4)
     )
     piece = dot(pick, absorbed).astype(BF16)
-    qslots[0, c] = piece[:, 0:256]
-    qslots[1, c] = piece[:, 256:512]
-
-    def slots(half, first, count=1):
-        return qslots.at[half, pl.ds(first, count)]
+    qslots[c] = piece
 
     dz_copies = {
-        o: go(
-            remote(qslots.at[:, c], qslots.at[:, c], dz_send.at[o], dz_recv.at[o], at_z(o))
-        )
-        for o in (4, 3, 5, 2, 6, 1, 7)
+        o: go(remote(qslots.at[c], qslots.at[c], dz_send.at[o], dz_recv.at[o], at_z(o))) for o in (1, 7, 2, 6, 3, 5, 4)
     }
-    early_copies, late_copies = [], []
+    dx_copies = []
     for k, i in enumerate((0, 1, 7, 2, 6, 3, 5, 4)):
         if i:
             dz_copies[i].wait_recv()
         slot = x * NZ + (z - i + NZ) % NZ
         for o in (2, 1, 3):
-            half = 1 - ((x + o) % NX) // 2
             n = k * 3 + o - 1
-            early_copies.append(
-                go(remote(slots(half, slot), slots(half, slot), dx_send.at[n], dx_recv.at[n], at_x(o)))
-            )
-    for o in (2, 1, 3):
-        half = ((x + o) % NX) // 2
-        n = 23 + o
-        late_copies.append(
-            go(
-                remote(
-                    slots(half, x * NZ, NZ), slots(half, x * NZ, NZ), dx_send.at[n], dx_recv.at[n], at_x(o)
-                )
-            )
-        )
-
-    copies[6].wait()
-    for copy in va_copies:
-        copy.wait_recv()
-    v3[r, :, z] = v1[:, z]
-    vb_copies = [
-        go(remote(v1.at[:, (z + o) % NZ], v3.at[r, :, z], v_send.at[3 + o], v_recv.at[3 + o], at_z(o)))
-        for o in range(1, NZ)
+            dx_copies.append(go(remote(qslots.at[slot], qslots.at[slot], dx_send.at[n], dx_recv.at[n], at_x(o))))
+
+    for copy in vb_copies:
+        copy.wait_recv()
+    vc_copies = [
+        go(remote(v3.at[r], v3.at[r], v_send.at[10 + o], v_recv.at[10 + o], at_y(o))) for o in range(1, NY)
     ]
+    take_apart(24, 64)
 
     copies[5].wait()
     row_of = iota((LAT, LAT), 0)
     line_up = ones_where(((row_of // 4) % 4) * 128 + (row_of // 16) * 4 + row_of % 4 == iota((LAT, LAT), 1))
+    for copy in dx_copies:
+        copy.wait_recv()
+    q[:, 0:LAT] = dot(qslots[...].reshape(LAT, ROWS), line_up, ((0,), (0,))).astype(BF16)
     f1_copies = []
     for i in range(NX):
-        o = (2, 3 - 2 * (x % 2), 1 + 2 * (x % 2), 0)[i]
-        if i % 2 == 0:
-            for copy in (late_copies if i else early_copies):
-                copy.wait_recv()
-            half = x // 2 if i else 1 - x // 2
-            gathered = dot(qslots[half].reshape(LAT, 256), line_up, ((0,), (0,)))
-            q[pl.ds(pl.multiple_of(half * 256, 256), 256), 0:LAT] = gathered.astype(BF16)
+        o = (2, 1, 3, 0)[i]
         g = (x + o) % NX
         rows = pl.ds(pl.multiple_of(g * GROUP, GROUP), GROUP)
         q_rows = q[rows, :]
@@ -294,13 +286,6 @@
         else:
             f1[x, :, 0:LAT] = weighted.astype(BF16)
             f1[x, :, LAT:WIDE] = pack_stats(top, total)
-        if i == 1:
-            for copy in vb_copies:
-                copy.wait_recv()
-            vc_copies = [
-                go(remote(v3.at[r], v3.at[r], v_send.at[10 + o], v_recv.at[10 + o], at_y(o)))
-                for o in range(1, NY)
-            ]
 
     for copy in f1_copies:
         copy.wait_recv()
@@ -319,7 +304,7 @@
         if o:
             f2_copies.append(go(remote(f2s.at[there], f2.at[z], f2_send.at[o], f2_recv.at[o], at_z(o))))
 
-    for i in (7, 8, 9, 10):
+    for i in (7, 8, 9, 10, 12):
         copies[i].wait()
     place = ones_where(iota((128, 8), 0) == iota((128, 8), 1))
     kr[512:640, :] = (dot(place[:, 0:4], nl[0]) + dot(place[:, 4:8], nl[1])).astype(BF16)
@@ -406,20 +391,19 @@
     new_rope,
 ):
     any_spec = pl.BlockSpec(memory_space=pl.ANY)
-    smem_spec = pl.BlockSpec(memory_space=pltpu.SMEM)
     dma = pltpu.SemaphoreType.DMA
     vmem = pltpu.VMEM
     summed = pl.pallas_call(
         kernel,
         out_shape=jax.ShapeDtypeStruct((8, 128), F32),
-        in_specs=[smem_spec] * 2 + [any_spec] * 11,
+        in_specs=[pl.BlockSpec(memory_space=pltpu.HBM)] * 2 + [any_spec] * 11,
         out_specs=pl.BlockSpec(memory_space=pltpu.VMEM),
         scratch_shapes=[
             vmem((ROWS, NOPE), BF16),
             vmem((ROWS, ROPE), BF16),
             vmem((ROWS, NOPE), BF16),
             vmem((NY, 256, NOPE), BF16),
-            vmem((2, NX * NZ, 16, 256), BF16),
+            vmem((NX * NZ, 16, ROWS), BF16),
             vmem((ROWS, WIDE), BF16),
             vmem((KEYS, LAT), BF16),
             vmem((WIDE, KEYS), BF16),
@@ -441,15 +425,17 @@
             vmem((NX, 2, NZ * 8, 128), BF16),
             vmem((NZ, 8, 128), F32),
             vmem((NZ, 8, 128), F32),
-            dma((11,)),
+            pltpu.SMEM((1,), jnp.int32),
+            pltpu.SMEM((1, 4), jnp.int32),
+            dma((13,)),
             dma((NY,)),
             dma((NY,)),
             dma((14,)),
             dma((14,)),
             dma((NZ,)),
             dma((NZ,)),
-            dma((27,)),
-            dma((27,)),
+            dma((24,)),
+            dma((24,)),
             dma((NX,)),
             dma((NX,)),
             dma((NZ,)),

time: 59.3 us -> 55.5 us (0.936)
  Pallas kernels: 57.2 us -> 53.4 us
    pallas_call x1, Pallas kernels: 57.2 us -> 53.4 us  [shards(): pl.pallas_call(kernel, out_shape=jax.ShapeDtypeStruct((8, 128), F32), in_...]
where the time goes in v3:
time: 55.5 us; the launch traced here: 55.3 us
  Pallas kernels  53.4 us (96%)
  other arithmetic  1.26 us (2%)
  between operations  0.66 us (1%)
    pallas_call x1, Pallas kernels, shards(): pl.pallas_call(kernel, out_shape=jax.ShapeDtypeStruct((8, 128), F32), in_...  53.4 us
    another operation x1, other arithmetic  1.26 us

profile of v3, /device:TPU:1, one launch (start us, length us, event | category | flops | bytes accessed | tf_op | source)
XLA Modules:
  0.0 55.3 jit_solution(8310297378173256226)
XLA Ops:
  0.7 53.4 %latent_attention.1 = f32[8,128]{1,0:T(8,128)} custom-call(s32[1]{0:T(128)S(6)} %copy.14.length_hbm, s32[1,4]{1,0:T(1,128)} %suffix_length_hbm.1, bf16[512,128]{1,0:T(8,128)(2,1)} %bitcast.19, bf16[512,64]{1,0:T(8,128)(2,1)} %bitcast.20, bf16[256,128]{1,0:T(8,128)(2,1)} %bitcast.21, bf16[4,8,8,128]{3,2,1,0:T(8,128)(2,1)} %bitcast.22, ...), custom_call_target="tpu_custom_call" | custom-call | tf_op jit(solution)/shard_map/latent_attention/pallas_call | solution.py:396
  54.1 1.3 %convert.3 = bf16[8,128]{1,0:T(8,128)(2,1)} convert(f32[8,128]{1,0:T(8,128)} %latent_attention.1) | non-fusion elementwise | flops 1024 | bytes 6144 | tf_op jit(solution)/shard_map/convert

commit v4 on v3

--- a/solution.py
+++ b/solution.py
@@ -150,14 +150,13 @@
         (suffix_length_hbm, suffix_length_ref),
     ]
     copies = [pltpu.make_async_copy(a, b, load_sem.at[i]) for i, (a, b) in enumerate(loads)]
-    for copy in copies:
-        copy.start()
-
     barrier = pltpu.get_barrier_semaphore()
     peers = [at_y(o) for o in range(1, NY)] + [at_x(o) for o in range(1, NX)]
     peers += [at_x(o, 1 - t) for o in range(NX)] + [at_z(o) for o in range(1, NZ)]
     for peer in peers:
         pl.semaphore_signal(barrier, inc=1, device_id=peer, device_id_type=MESH)
+    for i in (4, 6, 0, 1, 11, 2, 3, 5, 7, 8, 9, 10, 12):
+        copies[i].start()
 
     pl.semaphore_wait(barrier, len(peers))
 
@@ -304,6 +303,8 @@
         if o:
             f2_copies.append(go(remote(f2s.at[there], f2.at[z], f2_send.at[o], f2_recv.at[o], at_z(o))))
 
+    early_sends = sends[: -(NZ - 1)]
+
     for i in (7, 8, 9, 10, 12):
         copies[i].wait()
     place = ones_where(iota((128, 8), 0) == iota((128, 8), 1))
@@ -335,6 +336,9 @@
         pick = ones_where(iota((LAT, 1024), 1) == (latent // 4) * 8 + k * 4 + latent % 4)
         vde[:, k * 128 : (k + 1) * 128] = dot(pick, flat).astype(BF16)
 
+    for copy in early_sends:
+        copy.wait_send()
+
     for copy in f2_copies:
         copy.wait_recv()
     stats = [read_stats(f2[k, :, LAT:WIDE]) for k in range(NZ)]
@@ -371,7 +375,7 @@
         copy.wait_recv()
     out_ref[...] = jnp.sum(yz[...], axis=0)
 
-    for copy in sends:
+    for copy in sends[len(early_sends) :]:
         copy.wait_send()
 
 

time: 55.5 us -> 54.5 us (0.982)
  Pallas kernels: 53.4 us -> 52.5 us
    pallas_call x1, Pallas kernels: 53.4 us -> 52.5 us  [shards(): pl.pallas_call(kernel, out_shape=jax.ShapeDtypeStruct((8, 128), F32), in_...]
where the time goes in v4:
time: 54.5 us; the launch traced here: 54.4 us
  Pallas kernels  52.5 us (96%)
  other arithmetic  1.26 us (2%)
  between operations  0.66 us (1%)
    pallas_call x1, Pallas kernels, shards(): pl.pallas_call(kernel, out_shape=jax.ShapeDtypeStruct((8, 128), F32), in_...  52.5 us
    another operation x1, other arithmetic  1.26 us

profile of v4, /device:TPU:1, one launch (start us, length us, event | category | flops | bytes accessed | tf_op | source)
XLA Modules:
  0.0 54.4 jit_solution(9744224617771553103)
XLA Ops:
  0.7 52.5 %latent_attention.1 = f32[8,128]{1,0:T(8,128)} custom-call(s32[1]{0:T(128)S(6)} %copy.14.length_hbm, s32[1,4]{1,0:T(1,128)} %suffix_length_hbm.1, bf16[512,128]{1,0:T(8,128)(2,1)} %bitcast.19, bf16[512,64]{1,0:T(8,128)(2,1)} %bitcast.20, bf16[256,128]{1,0:T(8,128)(2,1)} %bitcast.21, bf16[4,8,8,128]{3,2,1,0:T(8,128)(2,1)} %bitcast.22, ...), custom_call_target="tpu_custom_call" | custom-call | tf_op jit(solution)/shard_map/latent_attention/pallas_call | solution.py:400
  53.1 1.3 %convert.3 = bf16[8,128]{1,0:T(8,128)(2,1)} convert(f32[8,128]{1,0:T(8,128)} %latent_attention.1) | non-fusion elementwise | flops 1024 | bytes 6144 | tf_op jit(solution)/shard_map/convert

commit v5 on v4

--- a/solution.py
+++ b/solution.py
@@ -74,6 +74,7 @@
     qn,
     qr,
     qnp,
+    own_head,
     kmg,
     qslots,
     q,
@@ -218,11 +219,12 @@
 
     take_apart(0, 24)
 
+    own_head[...] = jnp.where(iota((256, ROWS), 0) // 4 == iota((256, ROWS), 1) // 8, 1.0, 0.0)
+
     for copy in b_copies:
         copy.wait_recv()
     absorbed = dot(kmg[...].reshape(1024, NOPE), qnp[...], ((1,), (1,)))
-    own_head = (iota((1024, ROWS), 0) // 4) % 64 == iota((1024, ROWS), 1) // 8
-    absorbed = jnp.where(own_head, absorbed, 0.0).astype(BF16)
+    absorbed = (absorbed.reshape(NY, 256, ROWS) * own_head[...]).astype(BF16).reshape(1024, ROWS)
     pick = ones_where(
         (iota((16, 1024), 1) // 256 == iota((16, 1024), 0) // 4) & (iota((16, 1024), 1) % 4 == iota((16, 1024), 0) % 4)
     )
@@ -253,12 +255,12 @@
     line_up = ones_where(((row_of // 4) % 4) * 128 + (row_of // 16) * 4 + row_of % 4 == iota((LAT, LAT), 1))
     for copy in dx_copies:
         copy.wait_recv()
-    q[:, 0:LAT] = dot(qslots[...].reshape(LAT, ROWS), line_up, ((0,), (0,))).astype(BF16)
     f1_copies = []
     for i in range(NX):
         o = (2, 1, 3, 0)[i]
         g = (x + o) % NX
         rows = pl.ds(pl.multiple_of(g * GROUP, GROUP), GROUP)
+        q[rows, 0:LAT] = dot(qslots[:, :, rows].reshape(LAT, GROUP), line_up, ((0,), (0,))).astype(BF16)
         q_rows = q[rows, :]
         top = None
         for k in range(KEYS // 512):
@@ -406,6 +408,7 @@
             vmem((ROWS, NOPE), BF16),
             vmem((ROWS, ROPE), BF16),
             vmem((ROWS, NOPE), BF16),
+            vmem((256, ROWS), F32),
             vmem((NY, 256, NOPE), BF16),
             vmem((NX * NZ, 16, ROWS), BF16),
             vmem((ROWS, WIDE), BF16),

time: 54.5 us -> 54.6 us (level)
  no operation moved by 1% of the time
where the time goes in v5:
time: 54.6 us; the launch traced here: 54.5 us
  Pallas kernels  52.6 us (96%)
  other arithmetic  1.26 us (2%)
  between operations  0.66 us (1%)
    pallas_call x1, Pallas kernels, shards(): pl.pallas_call(kernel, out_shape=jax.ShapeDtypeStruct((8, 128), F32), in_...  52.6 us
    another operation x1, other arithmetic  1.26 us

profile of v5, /device:TPU:1, one launch (start us, length us, event | category | flops | bytes accessed | tf_op | source)
XLA Modules:
  0.0 54.5 jit_solution(7599233166522114964)
XLA Ops:
  0.7 52.6 %latent_attention.1 = f32[8,128]{1,0:T(8,128)} custom-call(s32[1]{0:T(128)S(6)} %copy.14.length_hbm, s32[1,4]{1,0:T(1,128)} %suffix_length_hbm.1, bf16[512,128]{1,0:T(8,128)(2,1)} %bitcast.19, bf16[512,64]{1,0:T(8,128)(2,1)} %bitcast.20, bf16[256,128]{1,0:T(8,128)(2,1)} %bitcast.21, bf16[4,8,8,128]{3,2,1,0:T(8,128)(2,1)} %bitcast.22, ...), custom_call_target="tpu_custom_call" | custom-call | tf_op jit(solution)/shard_map/latent_attention/pallas_call | solution.py:402
  53.3 1.3 %convert.3 = bf16[8,128]{1,0:T(8,128)(2,1)} convert(f32[8,128]{1,0:T(8,128)} %latent_attention.1) | non-fusion elementwise | flops 1024 | bytes 6144 | tf_op jit(solution)/shard_map/convert
